TPU v7x, 512 devices: a whole 4x4x16 slice. The times are simulated.
512 devices in a mesh: head: 8 (over x_lo, y), ctx: 64 (over x_hi, z, core).
Axes of the slice: x: 4 (x_hi: 2, x_lo: 2; x = x_hi * 2 + x_lo), y: 4, z: 16, core: 2. Of those that a mesh axis runs over, the one named last changes fastest.
Arguments:
- query_vectors: bfloat16 [8192, 4096], P('ctx', 'head'), may hold values from -120 to 120
- key_vectors: bfloat16 [8192, 1024], P('ctx', 'head'), may hold values from -8 to 8
- value_vectors: bfloat16 [8192, 1024], P('ctx', 'head'), may hold values from -6 to 6
- output_grad: bfloat16 [8192, 4096], P('ctx', 'head'), may hold values from -6 to 6
- out_weight: bfloat16 [4096, 4096], P('head', 'ctx'), may hold values from -0.09375 to 0.09375
- selected: int32 [8, 64, 3], P('head', 'ctx'), may hold values from 0 to 62, as said below
- counts: int32 [8, 64], P('head', 'ctx'), may hold values from 0 to 3, as said below
Outputs:
- query_grad: bfloat16 [8192, 4096], P('ctx', 'head')
- key_grad: bfloat16 [8192, 1024], P('ctx', 'head')
- value_grad: bfloat16 [8192, 1024], P('ctx', 'head')
Inputs may be any that keep to these rules, and one draw needn't show every extreme that they name: For block i >= 1, selected[g, i, 0] = i - 1 and the first min(3, i) entries are distinct blocks below i; further entries are 0. counts[g, i] <= min(3, i); the last block has 3 in every head group.
All inputs are finite; a program needn't handle non-finite values.
Results may differ from a plain program's by a relative error of at most 0.0075.
Values may be sent and summed in bfloat16 or wider, within the bound.
A program may use at most 64 MiB of HBM per device.

v0:
```python
import jax
import jax.numpy as jnp
from jax import lax
from jax.sharding import PartitionSpec as P

DH = 128


def partner_2(value, axis, apart):
    mask = 2**apart
    pairs = [(source, source ^ mask) for source in range(lax.axis_size(axis))]
    return lax.ppermute(value, axis, pairs)


def build_mask(slot_valid, block_rows):
    positions = jnp.arange(block_rows, dtype=jnp.int32)
    causal = positions[None, :] <= positions[:, None]
    groups, slot_count = slot_valid.shape
    own_part = causal[None]
    far_part = jnp.broadcast_to(slot_valid[:, :, None], (groups, slot_count, block_rows))
    far_part = far_part.reshape(groups, 1, slot_count * block_rows)
    far_part = jnp.broadcast_to(far_part, (groups, block_rows, slot_count * block_rows))
    return jnp.concatenate([own_part, far_part], axis=2)


def compact(member_mask, capacity):
    block_total = member_mask.shape[1]
    rank = jnp.cumsum(member_mask.astype(jnp.int32), axis=1) - 1
    slots = jnp.arange(capacity, dtype=jnp.int32)
    hits = member_mask[:, None, :] & (rank[:, None, :] == slots[None, :, None])
    valid = jnp.any(hits, axis=2)
    listed = jnp.sum(
        jnp.where(hits, jnp.arange(block_total, dtype=jnp.int32)[None, None, :], 0), axis=2
    )
    return (listed, valid, rank)


def lookup(table, listed):
    return jnp.take_along_axis(table, listed, axis=1)


def take_rows(buffer, index, keep):
    index = jnp.clip(index, 0, buffer.shape[1] - 1)
    rows = jnp.take_along_axis(buffer, index[:, :, None, None], axis=1)
    return jnp.where(keep[:, :, None, None], rows, jnp.zeros((), rows.dtype))


def body(query_vectors, key_vectors, value_vectors, output_grad, out_weight, selected, counts):
    block_rows = query_vectors.shape[0]
    head_width = query_vectors.shape[1]
    groups = key_vectors.shape[1] // DH
    group_size = head_width // key_vectors.shape[1]
    slot_count = selected.shape[2]
    ctx_size = lax.axis_size("ctx")
    levels = ctx_size.bit_length() - 1
    position = lax.axis_index("ctx")
    grad_rows = lax.all_gather(output_grad, "head", axis=1, tiled=True)
    head_grad = lax.dot_general(
        grad_rows,
        lax.all_gather(out_weight, "ctx", axis=1, tiled=True),
        (((1,), (1,)), ((), ())),
        preferred_element_type=jnp.float32,
    )
    head_grad = head_grad.astype(jnp.bfloat16)
    table_blocks, table_counts = (
        lax.all_gather(selected, "ctx", axis=1, tiled=True),
        lax.all_gather(counts, "ctx", axis=1, tiled=True),
    )
    block_ids = jnp.arange(ctx_size, dtype=jnp.int32)
    pair_block = table_blocks.reshape(groups, -1)
    pair_source = jnp.repeat(block_ids, slot_count)[None, :]
    pair_live = (
        jnp.arange(slot_count, dtype=jnp.int32)[None, None, :] < table_counts[:, :, None]
    ).reshape(groups, -1)
    all_bits = ctx_size - 1

    def member(device, fixed):
        agree = (
            ((pair_block ^ device) & fixed == 0)
            & ((pair_source ^ device) & (all_bits ^ fixed) == 0)
            & pair_live
        )
        return jnp.any(
            agree[:, :, None] & (pair_block[:, :, None] == block_ids[None, None, :]), axis=1
        )

    bit_order = list(reversed(range(levels)))
    fixed_masks = [
        sum((1 << number for number in bit_order[:section])) for section in range(levels + 1)
    ]
    chosen = selected[:, 0, :]
    slot_live = jnp.arange(slot_count, dtype=jnp.int32)[None, :] < counts[:, 0][:, None]
    own_keys = key_vectors.reshape(block_rows, groups, DH).transpose(1, 0, 2)[:, None]
    own_values = value_vectors.reshape(block_rows, groups, DH).transpose(1, 0, 2)[:, None]
    top_list, top_valid, held_rank = compact(member(position, fixed_masks[levels]), 1)
    held_keys = take_rows(own_keys, jnp.zeros_like(top_list), top_valid)
    held_values = take_rows(own_values, jnp.zeros_like(top_list), top_valid)
    for section in reversed(range(levels)):
        bit_number = bit_order[section]
        partner = position ^ 1 << bit_number
        own_bit = position >> bit_number & 1
        block_bit = block_ids >> bit_number & 1
        need_mine = member(position, fixed_masks[section])
        need_partner = member(partner, fixed_masks[section])
        give_mask = need_partner & (block_bit == own_bit)[None, :]
        take_mask = need_mine & (block_bit != own_bit)[None, :]
        send_capacity = min(slot_count * 2**section, 2 ** (levels - section - 1))
        give_list, give_valid, unused_rank = compact(give_mask, send_capacity)
        give_index = lookup(held_rank, give_list)
        got_keys, got_values = partner_2(
            (
                take_rows(held_keys, give_index, give_valid),
                take_rows(held_values, give_index, give_valid),
            ),
            "ctx",
            bit_number,
        )
        unused_list, unused_valid, take_rank = compact(take_mask, send_capacity)
        hold_capacity = min(slot_count * 2**section, 2 ** (levels - section))
        new_list, new_valid, new_rank = compact(need_mine, hold_capacity)
        near_side = new_list >> bit_number & 1 == own_bit
        from_self = new_valid & near_side
        from_peer = new_valid & jnp.logical_not(near_side)
        self_index = lookup(held_rank, new_list)
        peer_index = lookup(take_rank, new_list)
        held_keys = jnp.where(
            from_self[:, :, None, None],
            take_rows(held_keys, self_index, from_self),
            take_rows(got_keys, peer_index, from_peer),
        )
        held_values = jnp.where(
            from_self[:, :, None, None],
            take_rows(held_values, self_index, from_self),
            take_rows(got_values, peer_index, from_peer),
        )
        held_rank = new_rank
    far_index = lookup(held_rank, chosen)
    key_far = take_rows(held_keys, far_index, slot_live)
    value_far = take_rows(held_values, far_index, slot_live)
    key_all = jnp.concatenate([own_keys, key_far], axis=1).reshape(groups, -1, DH)
    value_all = jnp.concatenate([own_values, value_far], axis=1).reshape(groups, -1, DH)
    key_mask = build_mask(slot_live, block_rows)
    softmax_scale = DH ** (-0.5)

    def head_backward(carry, inputs):
        query_head, grad_head = inputs
        scores = (
            jnp.einsum("tgd,gkd->gtk", query_head, key_all, preferred_element_type=jnp.float32)
            * softmax_scale
        )
        masked = jnp.where(key_mask, scores, -jnp.inf)
        row_top = jnp.max(masked, axis=-1, keepdims=True)
        log_total = row_top + jnp.log(jnp.sum(jnp.exp(masked - row_top), axis=-1, keepdims=True))
        attn_probs = jnp.exp(masked - log_total)
        probs_low = attn_probs.astype(jnp.bfloat16)
        outputs = jnp.einsum(
            "gtk,gkd->tgd", probs_low, value_all, preferred_element_type=jnp.float32
        )
        delta_rows = jnp.sum(grad_head * outputs, axis=-1).T[..., None]
        grad_probs = jnp.einsum(
            "tgd,gkd->gtk", grad_head, value_all, preferred_element_type=jnp.float32
        )
        grad_scores = attn_probs * (grad_probs - delta_rows)
        scores_low = grad_scores.astype(jnp.bfloat16)
        query_part = jnp.einsum(
            "gtk,gkd->tgd", scores_low, key_all, preferred_element_type=jnp.float32
        )
        query_part = (query_part * softmax_scale).astype(jnp.bfloat16)
        value_part = jnp.einsum(
            "gtk,tgd->gkd", probs_low, grad_head, preferred_element_type=jnp.float32
        )
        key_part = (
            jnp.einsum("gtk,tgd->gkd", scores_low, query_head, preferred_element_type=jnp.float32)
            * softmax_scale
        )
        return ((carry[0] + key_part, carry[1] + value_part), query_part)

    query_heads = query_vectors.reshape(block_rows, groups, group_size, DH).transpose(2, 0, 1, 3)
    grad_heads = head_grad.reshape(block_rows, groups, group_size, DH).transpose(2, 0, 1, 3)
    empty_sum = jnp.zeros((groups, (slot_count + 1) * block_rows, DH), jnp.float32)
    (key_sum, value_sum), query_parts = lax.scan(
        head_backward, (empty_sum, empty_sum), (query_heads, grad_heads)
    )
    query_grad = query_parts.transpose(1, 2, 0, 3).reshape(block_rows, head_width)
    grad_order = list(range(levels))
    grad_fixed = [
        sum((1 << number for number in grad_order[:section])) for section in range(levels + 1)
    ]
    key_sum = key_sum.reshape(groups, slot_count + 1, block_rows, DH)
    value_sum = value_sum.reshape(groups, slot_count + 1, block_rows, DH)
    held_mask = member(position, 0)
    start_list, start_valid, held_rank = compact(held_mask, slot_count)
    match = (chosen[:, None, :] == start_list[:, :, None]) & slot_live[:, None, :]
    slot_of = jnp.sum(
        jnp.where(match, jnp.arange(slot_count, dtype=jnp.int32)[None, None, :], 0), axis=2
    )
    held_dkeys = take_rows(key_sum[:, 1:], slot_of, start_valid)
    held_dvalues = take_rows(value_sum[:, 1:], slot_of, start_valid)
    for section in range(levels):
        bit_number = grad_order[section]
        partner = position ^ 1 << bit_number
        own_bit = position >> bit_number & 1
        block_bit = block_ids >> bit_number & 1
        partner_mask = member(partner, grad_fixed[section])
        give_mask = held_mask & (block_bit != own_bit)[None, :]
        take_mask = partner_mask & (block_bit == own_bit)[None, :]
        send_capacity = min(slot_count * 2**section, 2 ** (levels - section - 1))
        give_list, give_valid, unused_rank = compact(give_mask, send_capacity)
        give_index = lookup(held_rank, give_list)
        got_dkeys, got_dvalues = partner_2(
            (
                take_rows(held_dkeys, give_index, give_valid),
                take_rows(held_dvalues, give_index, give_valid),
            ),
            "ctx",
            bit_number,
        )
        unused_list, unused_valid, take_rank = compact(take_mask, send_capacity)
        next_mask = held_mask & (block_bit == own_bit)[None, :] | take_mask
        hold_capacity = min(slot_count * 2 ** (section + 1), 2 ** (levels - section - 1))
        new_list, new_valid, new_rank = compact(next_mask, hold_capacity)
        keep_self = new_valid & lookup(held_mask, new_list)
        keep_peer = new_valid & lookup(take_mask, new_list)
        self_index = lookup(held_rank, new_list)
        peer_index = lookup(take_rank, new_list)
        held_dkeys = take_rows(held_dkeys, self_index, keep_self) + take_rows(
            got_dkeys, peer_index, keep_peer
        )
        held_dvalues = take_rows(held_dvalues, self_index, keep_self) + take_rows(
            got_dvalues, peer_index, keep_peer
        )
        held_mask = next_mask
        held_rank = new_rank
    key_total = key_sum[:, 0] + held_dkeys[:, 0]
    value_total = value_sum[:, 0] + held_dvalues[:, 0]
    key_grad = key_total.transpose(1, 0, 2).reshape(block_rows, groups * DH).astype(jnp.bfloat16)
    value_grad = (
        value_total.transpose(1, 0, 2).reshape(block_rows, groups * DH).astype(jnp.bfloat16)
    )
    return (query_grad, key_grad, value_grad)


def solution(mesh):
    placed = (
        P("ctx", "head"),
        P("ctx", "head"),
        P("ctx", "head"),
        P("ctx", "head"),
        P("head", "ctx"),
        P("head", "ctx", None),
        P("head", "ctx"),
    )
    return jax.shard_map(
        body,
        mesh=mesh,
        in_specs=placed,
        out_specs=(P("ctx", "head"), P("ctx", "head"), P("ctx", "head")),
        check_vma=False,
    )
```

profile of v0, /device:TPU:1, one launch (start us, length us, event | category | flops | bytes accessed | tf_op | source)
XLA Modules:
  0.0 558.2 jit_solution(5357940901036270)
XLA Ops:
  11.0 28.6 %all-reduce = s32[64]{0:T(128)S(1)} all-reduce(s32[64]{0:T(128)S(1)} %bitcast_dynamic-update-slice_fusion), channel_id=1, replica_groups=mesh['head'=8,'ctx'=64] {'ctx'}, use_global_device_ids=true, to_apply=%add | all-reduce | flops 64 | bytes 512
  42.5 76.3 %all_gather.16 = s32[1,64,3]{2,0,1:T(1,128)S(1)} all-gather(s32[1,1,3]{2,0,1:T(1,128)} %bitcast.2011), channel_id=1, replica_groups=mesh['head'=8,'ctx'=64] {'ctx'}, dimensions={1}, use_global_device_ids=true | all-gather | bytes 780 | tf_op jit(solution)/shard_map/all_gather | solution.py:66
  217.2 4.3 collective-permute-start.2
  224.1 5.8 %collective-permute-done.8 = bf16[1,4,128,128]{3,2,1,0:T(8,128)(2,1)S(1)} collective-permute-done((bf16[1,4,128,128]{3,2,1,0:T(8,128)(2,1)S(1)}, bf16[1,4,128,128]{3,2,1,0:T(8,128)(2,1)S(1)}, u32[]{:S(2)}, u32[]{:S(2)}) %collective-permute-start.8) | collective-permute-done | bytes 131104 | tf_op jit(solution)/shard_map/ppermute | solution.py:12
  237.7 7.5 %collective-permute-start.3 = (bf16[1,8,128,128]{3,2,1,0:T(8,128)(2,1)S(1)}, bf16[1,8,128,128]{3,2,1,0:T(8,128)(2,1)S(1)}, u32[]{:S(2)}, u32[]{:S(2)}) collective-permute-start(bf16[1,8,128,128]{3,2,1,0:T(8,128)(2,1)S(1)} %get-tuple-element.361), channel_id=1, source_target_pairs={{0,8},{1,9},{2,10},{3,11},{4,12},{5,13},{6,14},{7,15},{8,0},{9,1},... | collective-permute-start | bytes 786440 | tf_op jit(solution)/shard_map/ppermute | solution.py:12
  256.0 30.9 %collective-permute-done.9 = bf16[1,8,128,128]{3,2,1,0:T(8,128)(2,1)S(1)} collective-permute-done((bf16[1,8,128,128]{3,2,1,0:T(8,128)(2,1)S(1)}, bf16[1,8,128,128]{3,2,1,0:T(8,128)(2,1)S(1)}, u32[]{:S(2)}, u32[]{:S(2)}) %collective-permute-start.9) | collective-permute-done | bytes 262176 | tf_op jit(solution)/shard_map/ppermute | solution.py:12
  287.7 12.0 %collective-permute-done.3 = bf16[1,8,128,128]{3,2,1,0:T(8,128)(2,1)S(1)} collective-permute-done((bf16[1,8,128,128]{3,2,1,0:T(8,128)(2,1)S(1)}, bf16[1,8,128,128]{3,2,1,0:T(8,128)(2,1)S(1)}, u32[]{:S(2)}, u32[]{:S(2)}) %collective-permute-start.3) | collective-permute-done | bytes 262176 | tf_op jit(solution)/shard_map/ppermute | solution.py:12
  305.9 12.1 %collective-permute-start.4 = (bf16[1,6,128,128]{3,2,1,0:T(8,128)(2,1)S(1)}, bf16[1,6,128,128]{3,2,1,0:T(8,128)(2,1)S(1)}, u32[]{:S(2)}, u32[]{:S(2)}) collective-permute-start(bf16[1,6,128,128]{3,2,1,0:T(8,128)(2,1)S(1)} %get-tuple-element.359), channel_id=1, source_target_pairs={{0,16},{1,17},{2,18},{3,19},{4,20},{5,21},{6,22},{7,23},{8,24},{9,... | collective-permute-start | bytes 589832 | tf_op jit(solution)/shard_map/ppermute | solution.py:12
  322.3 10.3 %collective-permute-done.4 = bf16[1,6,128,128]{3,2,1,0:T(8,128)(2,1)S(1)} collective-permute-done((bf16[1,6,128,128]{3,2,1,0:T(8,128)(2,1)S(1)}, bf16[1,6,128,128]{3,2,1,0:T(8,128)(2,1)S(1)}, u32[]{:S(2)}, u32[]{:S(2)}) %collective-permute-start.4) | collective-permute-done | bytes 196640 | tf_op jit(solution)/shard_map/ppermute | solution.py:12
  337.6 4.9 collective-permute-start.5
  351.5 7.4 %while.22 = (s32[]{:T(128)}, f32[1,512,128]{2,1,0:T(8,128)S(1)}, f32[1,512,128]{2,1,0:T(8,128)S(1)}, bf16[4,128,1,128]{3,1,2,0:T(8,128)(2,1)S(1)}, pred[1,128,51...) while((s32[]{:T(128)}, f32[1,512,128]{2,1,0:T(8,128)S(1)}, ...), condition=%wide.region_61.79_spmd.clone, body=%wide.region_57.78_spmd.clone.sunk | while | flops 101924608 | bytes 3544728 | solution.py:181
  374.6 3.4 collective-permute-start.13
  380.1 4.8 collective-permute-done.19
  386.5 6.9 %collective-permute-done.13 = f32[1,6,128,128]{3,2,1,0:T(8,128)S(1)} collective-permute-done((f32[1,6,128,128]{3,2,1,0:T(8,128)S(1)}, f32[1,6,128,128]{3,2,1,0:T(8,128)S(1)}, u32[]{:S(2)}, u32[]{:S(2)}) %collective-permute-start.13) | collective-permute-done | bytes 393248 | tf_op jit(solution)/shard_map/ppermute | solution.py:12
  401.5 4.3 collective-permute-start.14
  407.3 31.5 %collective-permute-done.20 = f32[1,8,128,128]{3,2,1,0:T(8,128)S(1)} collective-permute-done((f32[1,8,128,128]{3,2,1,0:T(8,128)}, f32[1,8,128,128]{3,2,1,0:T(8,128)S(1)}, u32[]{:S(2)}, u32[]{:S(2)}) %collective-permute-start.20) | collective-permute-done | bytes 524320 | tf_op jit(solution)/shard_map/ppermute | solution.py:12
  441.3 8.9 %collective-permute-done.14 = f32[1,8,128,128]{3,2,1,0:T(8,128)} collective-permute-done((f32[1,8,128,128]{3,2,1,0:T(8,128)}, f32[1,8,128,128]{3,2,1,0:T(8,128)}, u32[]{:S(2)}, u32[]{:S(2)}) %collective-permute-start.14) | collective-permute-done | bytes 524320 | tf_op jit(solution)/shard_map/ppermute | solution.py:12
  457.3 7.3 %collective-permute-start.15 = (f32[1,4,128,128]{3,2,1,0:T(8,128)S(1)}, f32[1,4,128,128]{3,2,1,0:T(8,128)S(1)}, u32[]{:S(2)}, u32[]{:S(2)}) collective-permute-start(f32[1,4,128,128]{3,2,1,0:T(8,128)S(1)} %get-tuple-element.335), channel_id=1, source_target_pairs={{0,8},{1,9},{2,10},{3,11},{4,12},{5,13},{6,14},{7,15},{8,0},{9,1},... | collective-permute-start | bytes 786440 | tf_op jit(solution)/shard_map/ppermute | solution.py:12
  467.0 32.2 %collective-permute-done.21 = f32[1,4,128,128]{3,2,1,0:T(8,128)S(1)} collective-permute-done((f32[1,4,128,128]{3,2,1,0:T(8,128)S(1)}, f32[1,4,128,128]{3,2,1,0:T(8,128)S(1)}, u32[]{:S(2)}, u32[]{:S(2)}) %collective-permute-start.21) | collective-permute-done | bytes 262176 | tf_op jit(solution)/shard_map/ppermute | solution.py:12
  499.8 7.9 %collective-permute-done.15 = f32[1,4,128,128]{3,2,1,0:T(8,128)S(1)} collective-permute-done((f32[1,4,128,128]{3,2,1,0:T(8,128)S(1)}, f32[1,4,128,128]{3,2,1,0:T(8,128)S(1)}, u32[]{:S(2)}, u32[]{:S(2)}) %collective-permute-start.15) | collective-permute-done | bytes 262176 | tf_op jit(solution)/shard_map/ppermute | solution.py:12
  509.7 5.3 collective-permute-start.22
  515.0 8.7 %collective-permute-start.16 = (f32[1,2,128,128]{3,2,1,0:T(8,128)S(1)}, f32[1,2,128,128]{3,2,1,0:T(8,128)S(1)}, u32[]{:S(2)}, u32[]{:S(2)}) collective-permute-start(f32[1,2,128,128]{3,2,1,0:T(8,128)S(1)} %get-tuple-element.333), channel_id=1, source_target_pairs={{0,16},{1,17},{2,18},{3,19},{4,20},{5,21},{6,22},{7,23},{8,24},{9,... | collective-permute-start | bytes 393224 | tf_op jit(solution)/shard_map/ppermute | solution.py:12
  538.6 5.0 collective-permute-start.17
  546.8 3.9 collective-permute-done.23
  (688 shorter events, 207.1 us)
Async XLA Ops:
  7.2 340.8 %all-gather.3.cloned.1.call-start = ((), (), s32[]{:S(2)}) async-start(), calls=%async_computation | async-start | bytes 1179648 | tf_op jit(solution)/shard_map/all_gather | solution.py:57
  7.9 340.1 %all-gather.5.cloned.1.call-start = ((), (), s32[]{:S(2)}) async-start(), calls=%async_computation.1 | async-start | bytes 4259840 | tf_op jit(solution)/shard_map/all_gather | solution.py:60
  127.6 75.6 %collective-permute-start.6 = (bf16[1,1,128,128]{3,2,1,0:T(8,128)(2,1)S(1)}, bf16[1,1,128,128]{3,2,1,0:T(8,128)(2,1)S(1)}, u32[]{:S(2)}, u32[]{:S(2)}) collective-permute-start(bf16[1,1,128,128]{3,2,1,0:T(8,128)(2,1)S(1)} %get-tuple-element.287), channel_id=1, source_target_pairs={{0,1},{1,0},{2,3},{3,2},{4,5},{5,4},{6,7},{7,6},{8,9},{9,8},{10,11... | collective-permute-start | bytes 98312 | tf_op jit(solution)/shard_map/ppermute | solution.py:12
  131.8 71.4 %collective-permute-start = (bf16[1,1,128,128]{3,2,1,0:T(8,128)(2,1)S(1)}, bf16[1,1,128,128]{3,2,1,0:T(8,128)(2,1)S(1)}, u32[]{:S(2)}, u32[]{:S(2)}) collective-permute-start(bf16[1,1,128,128]{3,2,1,0:T(8,128)(2,1)S(1)} %get-tuple-element.289), channel_id=1, source_target_pairs={{0,1},{1,0},{2,3},{3,2},{4,5},{5,4},{6,7},{7,6},{8,9},{9,8},{10,11... | collective-permute-start | bytes 98312 | tf_op jit(solution)/shard_map/ppermute | solution.py:12
  204.6 6.5 %collective-permute-start.7 = (bf16[1,2,128,128]{3,2,1,0:T(8,128)(2,1)S(1)}, bf16[1,2,128,128]{3,2,1,0:T(8,128)(2,1)S(1)}, u32[]{:S(2)}, u32[]{:S(2)}) collective-permute-start(bf16[1,2,128,128]{3,2,1,0:T(8,128)(2,1)S(1)} %get-tuple-element.364), channel_id=1, source_target_pairs={{0,2},{1,3},{2,0},{3,1},{4,6},{5,7},{6,4},{7,5},{8,10},{9,11},{10,... | collective-permute-start | bytes 196616 | tf_op jit(solution)/shard_map/ppermute | solution.py:12
  215.3 14.6 %collective-permute-start.8 = (bf16[1,4,128,128]{3,2,1,0:T(8,128)(2,1)S(1)}, bf16[1,4,128,128]{3,2,1,0:T(8,128)(2,1)S(1)}, u32[]{:S(2)}, u32[]{:S(2)}) collective-permute-start(bf16[1,4,128,128]{3,2,1,0:T(8,128)(2,1)S(1)} %get-tuple-element.362), channel_id=1, source_target_pairs={{0,4},{1,5},{2,6},{3,7},{4,0},{5,1},{6,2},{7,3},{8,12},{9,13},{10,... | collective-permute-start | bytes 393224 | tf_op jit(solution)/shard_map/ppermute | solution.py:12
  217.2 16.4 %collective-permute-start.2 = (bf16[1,4,128,128]{3,2,1,0:T(8,128)(2,1)S(1)}, bf16[1,4,128,128]{3,2,1,0:T(8,128)(2,1)S(1)}, u32[]{:S(2)}, u32[]{:S(2)}) collective-permute-start(bf16[1,4,128,128]{3,2,1,0:T(8,128)(2,1)S(1)} %get-tuple-element.363), channel_id=1, source_target_pairs={{0,4},{1,5},{2,6},{3,7},{4,0},{5,1},{6,2},{7,3},{8,12},{9,13},{10,... | collective-permute-start | bytes 393224 | tf_op jit(solution)/shard_map/ppermute | solution.py:12
  235.8 51.2 %collective-permute-start.9 = (bf16[1,8,128,128]{3,2,1,0:T(8,128)(2,1)S(1)}, bf16[1,8,128,128]{3,2,1,0:T(8,128)(2,1)S(1)}, u32[]{:S(2)}, u32[]{:S(2)}) collective-permute-start(bf16[1,8,128,128]{3,2,1,0:T(8,128)(2,1)S(1)} %get-tuple-element.360), channel_id=1, source_target_pairs={{0,8},{1,9},{2,10},{3,11},{4,12},{5,13},{6,14},{7,15},{8,0},{9,1},... | collective-permute-start | bytes 786440 | tf_op jit(solution)/shard_map/ppermute | solution.py:12
  237.7 62.0 %collective-permute-start.3 = (bf16[1,8,128,128]{3,2,1,0:T(8,128)(2,1)S(1)}, bf16[1,8,128,128]{3,2,1,0:T(8,128)(2,1)S(1)}, u32[]{:S(2)}, u32[]{:S(2)}) collective-permute-start(bf16[1,8,128,128]{3,2,1,0:T(8,128)(2,1)S(1)} %get-tuple-element.361), channel_id=1, source_target_pairs={{0,8},{1,9},{2,10},{3,11},{4,12},{5,13},{6,14},{7,15},{8,0},{9,1},... | collective-permute-start | bytes 786440 | tf_op jit(solution)/shard_map/ppermute | solution.py:12
  303.9 17.6 %collective-permute-start.10 = (bf16[1,6,128,128]{3,2,1,0:T(8,128)(2,1)S(1)}, bf16[1,6,128,128]{3,2,1,0:T(8,128)(2,1)S(1)}, u32[]{:S(2)}, u32[]{:S(2)}) collective-permute-start(bf16[1,6,128,128]{3,2,1,0:T(8,128)(2,1)S(1)} %get-tuple-element.358), channel_id=1, source_target_pairs={{0,16},{1,17},{2,18},{3,19},{4,20},{5,21},{6,22},{7,23},{8,24},{9,... | collective-permute-start | bytes 589832 | tf_op jit(solution)/shard_map/ppermute | solution.py:12
  305.9 26.7 %collective-permute-start.4 = (bf16[1,6,128,128]{3,2,1,0:T(8,128)(2,1)S(1)}, bf16[1,6,128,128]{3,2,1,0:T(8,128)(2,1)S(1)}, u32[]{:S(2)}, u32[]{:S(2)}) collective-permute-start(bf16[1,6,128,128]{3,2,1,0:T(8,128)(2,1)S(1)} %get-tuple-element.359), channel_id=1, source_target_pairs={{0,16},{1,17},{2,18},{3,19},{4,20},{5,21},{6,22},{7,23},{8,24},{9,... | collective-permute-start | bytes 589832 | tf_op jit(solution)/shard_map/ppermute | solution.py:12
  335.7 8.2 %collective-permute-start.11 = (bf16[1,3,128,128]{3,2,1,0:T(8,128)(2,1)S(1)}, bf16[1,3,128,128]{3,2,1,0:T(8,128)(2,1)S(1)}, u32[]{:S(2)}, u32[]{:S(2)}) collective-permute-start(bf16[1,3,128,128]{3,2,1,0:T(8,128)(2,1)S(1)} %get-tuple-element.356), channel_id=1, source_target_pairs={{0,32},{1,33},{2,34},{3,35},{4,36},{5,37},{6,38},{7,39},{8,40},{9,... | collective-permute-start | bytes 294920 | tf_op jit(solution)/shard_map/ppermute | solution.py:12
  337.6 8.0 %collective-permute-start.5 = (bf16[1,3,128,128]{3,2,1,0:T(8,128)(2,1)S(1)}, bf16[1,3,128,128]{3,2,1,0:T(8,128)(2,1)S(1)}, u32[]{:S(2)}, u32[]{:S(2)}) collective-permute-start(bf16[1,3,128,128]{3,2,1,0:T(8,128)(2,1)S(1)} %get-tuple-element.357), channel_id=1, source_target_pairs={{0,32},{1,33},{2,34},{3,35},{4,36},{5,37},{6,38},{7,39},{8,40},{9,... | collective-permute-start | bytes 294920 | tf_op jit(solution)/shard_map/ppermute | solution.py:12
  362.0 6.7 %collective-permute-start.18 = (f32[1,3,128,128]{3,2,1,0:T(8,128)S(1)}, f32[1,3,128,128]{3,2,1,0:T(8,128)S(1)}, u32[]{:S(2)}, u32[]{:S(2)}) collective-permute-start(f32[1,3,128,128]{3,2,1,0:T(8,128)S(1)} %get-tuple-element.340), channel_id=1, source_target_pairs={{0,1},{1,0},{2,3},{3,2},{4,5},{5,4},{6,7},{7,6},{8,9},{9,8},{10,11... | collective-permute-start | bytes 589832 | tf_op jit(solution)/shard_map/ppermute | solution.py:12
  372.7 12.3 %collective-permute-start.19 = (f32[1,6,128,128]{3,2,1,0:T(8,128)}, f32[1,6,128,128]{3,2,1,0:T(8,128)S(1)}, u32[]{:S(2)}, u32[]{:S(2)}) collective-permute-start(f32[1,6,128,128]{3,2,1,0:T(8,128)} %get-tuple-element.338), channel_id=1, source_target_pairs={{0,2},{1,3},{2,0},{3,1},{4,6},{5,7},{6,4},{7,5},{8,10},{9,11},{10,... | collective-permute-start | bytes 1179656 | tf_op jit(solution)/shard_map/ppermute | solution.py:12
  374.6 18.8 %collective-permute-start.13 = (f32[1,6,128,128]{3,2,1,0:T(8,128)S(1)}, f32[1,6,128,128]{3,2,1,0:T(8,128)S(1)}, u32[]{:S(2)}, u32[]{:S(2)}) collective-permute-start(f32[1,6,128,128]{3,2,1,0:T(8,128)S(1)} %get-tuple-element.339), channel_id=1, source_target_pairs={{0,2},{1,3},{2,0},{3,1},{4,6},{5,7},{6,4},{7,5},{8,10},{9,11},{10,... | collective-permute-start | bytes 1179656 | tf_op jit(solution)/shard_map/ppermute | solution.py:12
  399.6 39.3 %collective-permute-start.20 = (f32[1,8,128,128]{3,2,1,0:T(8,128)}, f32[1,8,128,128]{3,2,1,0:T(8,128)S(1)}, u32[]{:S(2)}, u32[]{:S(2)}) collective-permute-start(f32[1,8,128,128]{3,2,1,0:T(8,128)} %get-tuple-element.336), channel_id=1, source_target_pairs={{0,4},{1,5},{2,6},{3,7},{4,0},{5,1},{6,2},{7,3},{8,12},{9,13},{10,... | collective-permute-start | bytes 1572872 | tf_op jit(solution)/shard_map/ppermute | solution.py:12
  401.5 48.7 %collective-permute-start.14 = (f32[1,8,128,128]{3,2,1,0:T(8,128)}, f32[1,8,128,128]{3,2,1,0:T(8,128)}, u32[]{:S(2)}, u32[]{:S(2)}) collective-permute-start(f32[1,8,128,128]{3,2,1,0:T(8,128)} %get-tuple-element.337), channel_id=1, source_target_pairs={{0,4},{1,5},{2,6},{3,7},{4,0},{5,1},{6,2},{7,3},{8,12},{9,13},{10,... | collective-permute-start | bytes 1572872 | tf_op jit(solution)/shard_map/ppermute | solution.py:12
  455.4 43.9 %collective-permute-start.21 = (f32[1,4,128,128]{3,2,1,0:T(8,128)S(1)}, f32[1,4,128,128]{3,2,1,0:T(8,128)S(1)}, u32[]{:S(2)}, u32[]{:S(2)}) collective-permute-start(f32[1,4,128,128]{3,2,1,0:T(8,128)S(1)} %get-tuple-element.334), channel_id=1, source_target_pairs={{0,8},{1,9},{2,10},{3,11},{4,12},{5,13},{6,14},{7,15},{8,0},{9,1},... | collective-permute-start | bytes 786440 | tf_op jit(solution)/shard_map/ppermute | solution.py:12
  457.3 50.4 %collective-permute-start.15 = (f32[1,4,128,128]{3,2,1,0:T(8,128)S(1)}, f32[1,4,128,128]{3,2,1,0:T(8,128)S(1)}, u32[]{:S(2)}, u32[]{:S(2)}) collective-permute-start(f32[1,4,128,128]{3,2,1,0:T(8,128)S(1)} %get-tuple-element.335), channel_id=1, source_target_pairs={{0,8},{1,9},{2,10},{3,11},{4,12},{5,13},{6,14},{7,15},{8,0},{9,1},... | collective-permute-start | bytes 786440 | tf_op jit(solution)/shard_map/ppermute | solution.py:12
  509.7 26.9 %collective-permute-start.22 = (f32[1,2,128,128]{3,2,1,0:T(8,128)S(1)}, f32[1,2,128,128]{3,2,1,0:T(8,128)S(1)}, u32[]{:S(2)}, u32[]{:S(2)}) collective-permute-start(f32[1,2,128,128]{3,2,1,0:T(8,128)S(1)} %get-tuple-element.332), channel_id=1, source_target_pairs={{0,16},{1,17},{2,18},{3,19},{4,20},{5,21},{6,22},{7,23},{8,24},{9,... | collective-permute-start | bytes 393224 | tf_op jit(solution)/shard_map/ppermute | solution.py:12
  515.0 22.2 %collective-permute-start.16 = (f32[1,2,128,128]{3,2,1,0:T(8,128)S(1)}, f32[1,2,128,128]{3,2,1,0:T(8,128)S(1)}, u32[]{:S(2)}, u32[]{:S(2)}) collective-permute-start(f32[1,2,128,128]{3,2,1,0:T(8,128)S(1)} %get-tuple-element.333), channel_id=1, source_target_pairs={{0,16},{1,17},{2,18},{3,19},{4,20},{5,21},{6,22},{7,23},{8,24},{9,... | collective-permute-start | bytes 393224 | tf_op jit(solution)/shard_map/ppermute | solution.py:12
  538.6 7.5 %collective-permute-start.17 = (f32[1,1,128,128]{3,2,1,0:T(8,128)S(1)}, f32[1,1,128,128]{3,2,1,0:T(8,128)S(1)}, u32[]{:S(2)}, u32[]{:S(2)}) collective-permute-start(f32[1,1,128,128]{3,2,1,0:T(8,128)S(1)} %select_select_fusion.2), channel_id=1, source_target_pairs={{0,32},{1,33},{2,34},{3,35},{4,36},{5,37},{6,38},{7,39},{8,40},{9,... | collective-permute-start | bytes 196616 | tf_op jit(solution)/shard_map/ppermute | solution.py:12
  544.2 6.5 %collective-permute-start.23 = (f32[1,1,128,128]{3,2,1,0:T(8,128)S(1)}, f32[1,1,128,128]{3,2,1,0:T(8,128)S(1)}, u32[]{:S(2)}, u32[]{:S(2)}) collective-permute-start(f32[1,1,128,128]{3,2,1,0:T(8,128)S(1)} %select_select_fusion), channel_id=1, source_target_pairs={{0,32},{1,33},{2,34},{3,35},{4,36},{5,37},{6,38},{7,39},{8,40},{9,... | collective-permute-start | bytes 196616 | tf_op jit(solution)/shard_map/ppermute | solution.py:12
  (65 other events, 2394.5 us)
Sparse Core Ops, SparseCore 0:
  10.1 47.0 all-gather.2
  134.3 192.3 all-gather.4
where the time goes:
time: 561 us; the launch traced here: 558 us
  waiting for transfers between devices  163 us (29%)
  blocking collectives  105 us (19%)
  starting transfers between devices  92.9 us (17%)
  local copies, waits for them, and re-layouts  87.8 us (16%)
  other arithmetic  71.4 us (13%)
  between operations  28.2 us (5%)
  matrix products  9.57 us (2%)
    ppermute x24, waiting for transfers between devices, partner_2(): return lax.ppermute(value, axis, pairs)  162 us
    ppermute x24, starting transfers between devices, partner_2(): return lax.ppermute(value, axis, pairs)  92.8 us
    all_gather x1, blocking collectives, body(): lax.all_gather(selected, 'ctx', axis=1, tiled=True)  76.3 us
    gather x64, local copies, waits for them, and re-layouts, take_rows(): rows = jnp.take_along_axis(buffer, index[:, :, None, None], axis=1)  46.3 us
    gather x44, local copies, waits for them, and re-layouts, lookup(): return jnp.take_along_axis(table, listed, axis=1)  32.1 us
    unnamed x1, blocking collectives  28.6 us
    reduce_or x24, other arithmetic, compact(): valid = jnp.any(hits, axis=2)  11.5 us
  transfers between devices with their start and end apart: 26, of which 15 were waited for; matrix products, arithmetic and copies ran while one was open for 24% of the time, Pallas kernels for 0%

commit v1 on v0

v1 whole, which is shorter than its diff:
```python
import functools

import jax
import jax.numpy as jnp
from jax import lax
from jax.experimental import pallas as pl
from jax.experimental.pallas import tpu as pltpu
from jax.sharding import PartitionSpec as P

MESH = pl.DeviceIdType.MESH
DH = 128
NEG = -1e30
AG_K = 1
RS_K = 2
F32 = jnp.float32
BF16 = jnp.bfloat16


def dot(a, b, dims):
    return lax.dot_general(a, b, (dims, ((), ())), preferred_element_type=F32)


NN = ((1,), (0,))
NT = ((1,), (1,))


def kernel(
    ny, nz,
    q_ref, k_ref, v_ref, og_ref, w_ref, sel_ref, cnt_ref,
    dq_ref, dk_ref, dv_ref,
    kvbuf, wbuf, ogbuf, stage, tiles, ids, csend, crecv,
    kall, vall, pfull, plow, dslow, do4, q4, own_sum, pslot, s0buf, s0r, sbuf, rbuf,
    kv_s, kv_r, kvc_s, kvc_r, w_s, w_r, wc_s, wc_r, ogx_s, ogx_r, ogy_s, ogy_r,
    tile_s, tile_r, ids_s, kvx_s, kvx_r, c_s, c_r, sl_s, sl_r, s0_s, s0_r, rs_s, rs_r,
):
    lane = 2 * nz
    head, ctx = lax.axis_index("head"), lax.axis_index("ctx")
    xl, y = head // ny, head % ny
    xh, z, c = ctx // lane, (ctx // 2) % nz, ctx % 2
    rows = q_ref.shape[0]
    width = q_ref.shape[1]
    heads = width // DH
    half = [nz // 2, nz // 2 - 1]

    def zdev(step):
        return (head, xh * lane + ((z + step + nz) % nz) * 2 + c)

    core_dev = (head, xh * lane + z * 2 + (1 - c))
    x_dev = (head, (1 - xh) * lane + z * 2 + c)
    xc_dev = (head, (1 - xh) * lane + z * 2 + (1 - c))
    prev_dev = (head, (ctx + 2 * lane - 1) % (2 * lane))
    next_dev = (head, (ctx + 1) % (2 * lane))

    def remote(src, dst, send, recv, dev):
        return pltpu.make_async_remote_copy(
            src_ref=src, dst_ref=dst, send_sem=send, recv_sem=recv, device_id=dev, device_id_type=MESH
        )

    barrier = pltpu.get_barrier_semaphore()
    greet = [core_dev, x_dev, xc_dev, prev_dev, next_dev]
    greet += [((1 - xl) * ny + y, ctx), ((1 - xl) * ny + y, (1 - xh) * lane + z * 2 + c)]
    greet += [(xl * ny + (y + dy) % ny, ctx) for dy in range(1, ny)]
    greet += [zdev(sg * k) for k in range(1, max(AG_K, RS_K) + 1) for sg in (1, -1)]
    for dev in greet:
        pl.semaphore_signal(barrier, inc=1, device_id=dev, device_id_type=MESH)

    me = z * 2 + c
    kvbuf[me, 0:rows] = k_ref[...]
    kvbuf[me, rows : 2 * rows] = v_ref[...]
    row_id = lax.broadcasted_iota(jnp.int32, (8, 128), 0)
    tiles[0] = jnp.where(row_id == 0, sel_ref[0, 0, 1], sel_ref[0, 0, 2])
    pl.semaphore_wait(barrier, len(greet))

    def ring(buf, send, recv, dr, off, k):
        sg = 1 if dr == 0 else -1
        slot = ((z - sg * off + nz) % nz) * 2 + c
        return remote(
            buf.at[slot], buf.at[slot], send.at[dr, off + k - 1], recv.at[dr, off + k - 1], zdev(sg * k)
        )

    def to_core(buf, send, recv, slot_z):
        slot = slot_z * 2 + c
        return remote(buf.at[slot], buf.at[slot], send.at[slot_z], recv.at[slot_z], core_dev)

    started = []

    def relay(buf, sems, dr, off):
        send, recv, csnd, crcv = sems
        for k in range(AG_K, 0, -1):
            if off + k <= half[dr]:
                cp = ring(buf, send, recv, dr, off, k)
                cp.start()
                started.append(cp)
        if not (off == 0 and dr == 1):
            sg = 1 if dr == 0 else -1
            cp = to_core(buf, csnd, crcv, (z - sg * off + nz) % nz)
            cp.start()
            started.append(cp)

    def arrived(buf, sems, dr, off):
        ring(buf, sems[0], sems[1], dr, off - 1, 1).wait_recv()

    kv_sems = (kv_s, kv_r, kvc_s, kvc_r)
    w_sems = (w_s, w_r, wc_s, wc_r)
    relay(kvbuf, kv_sems, 0, 0)
    relay(kvbuf, kv_sems, 1, 0)
    wbuf[me] = w_ref[...].T
    relay(wbuf, w_sems, 0, 0)
    relay(wbuf, w_sems, 1, 0)

    tile_cps = [
        remote(tiles.at[0], tiles.at[n], tile_s.at[n - 1], tile_r.at[n - 1], dev)
        for n, dev in ((1, core_dev), (2, x_dev), (3, xc_dev))
    ]
    for cp in tile_cps:
        cp.start()

    ogx = [
        remote(og_ref, ogbuf.at[xh, y], ogx_s.at[t], ogx_r.at[xh], (t * ny + y, xl * lane + z * 2 + c))
        for t in range(2)
    ]
    for t in range(2):
        @pl.when(jnp.logical_not((xh == xl) & (xl == t)))
        def _():
            ogx[t].start()

    @pl.when(xh == xl)
    def _():
        ogbuf[xh, y] = og_ref[...]

    for h in range(heads):
        q4[h * rows : (h + 1) * rows] = q_ref[:, h * DH : (h + 1) * DH]
    for n in range(4):
        pslot[n, 2] = jnp.zeros(pslot.shape[2:], BF16)

    def ogy(b, dy, slot_y):
        return remote(
            ogbuf.at[b, slot_y], ogbuf.at[b, slot_y], ogy_s.at[b, dy - 1], ogy_r.at[b, dy - 1],
            (xl * ny + (y + dy) % ny, ctx),
        )

    def ogx_done():
        for b in range(2):
            @pl.when(jnp.logical_not((xh == b) & (xl == b)))
            def _():
                remote(og_ref, ogbuf.at[b, y], ogx_s.at[0], ogx_r.at[b], x_dev).wait_recv()
        for b in range(2):
            for dy in range(1, ny):
                ogy(b, dy, y).start()

    for off in range(1, half[0] + 1):
        for buf, sems in ((kvbuf, kv_sems), (wbuf, w_sems)):
            for dr in (0, 1):
                if off <= half[dr]:
                    arrived(buf, sems, dr, off)
                    relay(buf, sems, dr, off)
        if off == 2:
            ogx_done()
        if off == 3:
            for cp in tile_cps:
                cp.wait_recv()
            to_ids = pltpu.make_async_copy(tiles, ids, ids_s)
            to_ids.start()
            to_ids.wait()

    def core_wait(buf, sems):
        for slot_z in range(nz):
            slot = slot_z * 2 + (1 - c)
            remote(buf.at[slot], buf.at[slot], sems[2].at[slot_z], sems[3].at[slot_z], core_dev).wait_recv()

    core_wait(kvbuf, kv_sems)

    kvx = [remote(stage.at[n], kvbuf.at[lane + n], kvx_s.at[n], kvx_r.at[n], x_dev) for n in range(3)]
    first = (z == 0) & (c == 0)

    @pl.when(xh == 0)
    def _():
        for n in (1, 2):
            stage[n] = kvbuf[jnp.clip(ids[2, n - 1, 0], 0, lane - 1)]
            kvx[n].start()

        @pl.when(first)
        def _():
            stage[0] = kvbuf[lane - 1]
            kvx[0].start()

    core_wait(wbuf, w_sems)
    for b in range(2):
        for dy in range(1, ny):
            ogy(b, dy, (y - dy + ny) % ny).wait_recv()

    per = lane // ny

    def project(b):
        total = None
        for part in range(ny):
            weight = wbuf[part * per : (part + 1) * per].reshape(-1, width)
            term = dot(ogbuf[b, part], weight, NN)
            total = term if total is None else total + term
        return total

    csend[...] = project(1 - xh).astype(BF16)
    cx = remote(csend, crecv, c_s, c_r, x_dev)
    cx.start()
    own_part = project(xh)

    @pl.when(xh == 1)
    def _():
        for n in (1, 2):
            kvx[n].wait_recv()

        @pl.when(first)
        def _():
            kvx[0].wait_recv()

    kall[0:rows] = k_ref[...]
    vall[0:rows] = v_ref[...]
    for n in range(3):
        b = sel_ref[0, 0, n]
        near = jnp.clip(b - xh * lane, 0, lane - 1)
        block = kvbuf[jnp.where(b >= xh * lane, near, lane + n)]
        kall[(n + 1) * rows : (n + 2) * rows] = block[0:rows]
        vall[(n + 1) * rows : (n + 2) * rows] = block[rows : 2 * rows]

    scale = DH ** -0.5
    count = cnt_ref[0, 0]
    key_pos = lax.broadcasted_iota(jnp.int32, (rows, rows), 0)
    tok_pos = lax.broadcasted_iota(jnp.int32, (rows, rows), 1)
    for h in range(heads):
        part = dot(kall[...], q_ref[:, h * DH : (h + 1) * DH], NT) * scale
        pieces = [jnp.where(key_pos <= tok_pos, part[0:rows], NEG)]
        for n in range(3):
            pieces.append(part[(n + 1) * rows : (n + 2) * rows] + jnp.where(n < count, 0.0, NEG))
        scores = jnp.concatenate(pieces, axis=0)
        top = jnp.max(scores, axis=0, keepdims=True)
        raised = jnp.exp(scores - top)
        probs = raised * (1.0 / jnp.sum(raised, axis=0, keepdims=True))
        pfull[h] = probs
        plow[:, h * rows : (h + 1) * rows] = probs.astype(BF16)

    cx.wait_recv()
    head_grad = (own_part + crecv[...].astype(F32)).astype(BF16)
    for h in range(heads):
        do4[h * rows : (h + 1) * rows] = head_grad[:, h * DH : (h + 1) * DH]
    for h in range(heads):
        grad_probs = dot(vall[...], do4[h * rows : (h + 1) * rows], NT)
        low = plow[:, h * rows : (h + 1) * rows].astype(F32)
        delta = jnp.sum(low * grad_probs, axis=0, keepdims=True)
        dslow[:, h * rows : (h + 1) * rows] = (pfull[h] * (grad_probs - delta)).astype(BF16)

    dv_all = dot(plow[...], do4[...], NN)
    dk_all = dot(dslow[...], q4[...], NN)
    own_sum[0:rows] = dk_all[0:rows]
    own_sum[rows : 2 * rows] = dv_all[0:rows]
    for n in (1, 2):
        pslot[0, n - 1, 0:rows] = dk_all[(n + 1) * rows : (n + 2) * rows].astype(BF16)
        pslot[0, n - 1, rows : 2 * rows] = dv_all[(n + 1) * rows : (n + 2) * rows].astype(BF16)

    def slots(src, dst, n, dev):
        return remote(
            pslot.at[src, pl.ds(0, 2)], pslot.at[dst, pl.ds(0, 2)], sl_s.at[n], sl_r.at[n], dev
        )

    sl_x = slots(0, 2, 1, x_dev)
    sl_c = slots(0, 1, 0, core_dev)
    sl_f = slots(2, 3, 2, core_dev)

    @pl.when(xh == 1)
    def _():
        sl_x.start()

    sl_c.start()
    s0buf[0:rows] = dk_all[rows : 2 * rows].astype(BF16)
    s0buf[rows : 2 * rows] = dv_all[rows : 2 * rows].astype(BF16)
    s0 = remote(s0buf, s0r, s0_s, s0_r, prev_dev)

    @pl.when(ctx > 0)
    def _():
        s0.start()

    key_t = kall[...].T
    for h in range(heads):
        part = dot(key_t, dslow[:, h * rows : (h + 1) * rows], NN) * scale
        dq_ref[:, h * DH : (h + 1) * DH] = part.T.astype(BF16)

    sl_c.wait_recv()

    @pl.when(xh == 0)
    def _():
        sl_x.wait_recv()
        sl_f.start()
        sl_f.wait_recv()

    wanted = [(sel_ref[0, 0, 1], sel_ref[0, 0, 2])] + [(ids[n, 0, 0], ids[n, 1, 0]) for n in (1, 2, 3)]

    def contribution(slot_z):
        target = xh * lane + slot_z * 2 + c
        total = None
        for n, (one, two) in enumerate(wanted):
            index = jnp.where(one == target, 0, jnp.where(two == target, 1, 2))
            term = pslot[n, index].astype(F32)
            total = term if total is None else total + term
        return total

    def rs_copy(dr, o):
        sg = 1 if dr == 0 else -1
        r = o % RS_K or RS_K
        return remote(sbuf.at[dr, o - 1], rbuf.at[dr, o - 1], rs_s.at[dr, o - 1], rs_r.at[dr, o - 1], zdev(sg * r))

    def rs_collect(total, dr, o):
        for o2 in range(o + 1, min(o + RS_K, half[dr]) + 1):
            rs_copy(dr, o2).wait_recv()
            total = total + rbuf[dr, o2 - 1].astype(F32)
        return total

    def rs_send(dr, o):
        sg = 1 if dr == 0 else -1
        total = contribution((z + sg * o + nz) % nz)
        if o % RS_K == 0:
            total = rs_collect(total, dr, o)
        sbuf[dr, o - 1] = total.astype(BF16)
        rs_copy(dr, o).start()

    order = sorted(
        ((dr, o) for dr in (0, 1) for o in range(1, half[dr] + 1)),
        key=lambda m: (-(m[1] if m[1] % RS_K == 0 else m[1] + RS_K + 0.5), m[0]),
    )
    for dr, o in order:
        rs_send(dr, o)
    total = own_sum[...] + contribution(z)

    @pl.when(ctx < 2 * lane - 1)
    def _():
        s0.wait_recv()

    total = total + jnp.where(ctx < 2 * lane - 1, s0r[...].astype(F32), 0.0)
    for dr in (0, 1):
        total = rs_collect(total, dr, 0)
    dk_ref[...] = (total[0:rows] * scale).astype(BF16)
    dv_ref[...] = total[rows : 2 * rows].astype(BF16)

    for cp in started:
        cp.wait_send()
    for cp in tile_cps:
        cp.wait_send()
    for t in range(2):
        @pl.when(jnp.logical_not((xh == xl) & (xl == t)))
        def _():
            ogx[t].wait_send()
    for b in range(2):
        for dy in range(1, ny):
            ogy(b, dy, y).wait_send()
    cx.wait_send()
    sl_c.wait_send()

    @pl.when(xh == 0)
    def _():
        for n in (1, 2):
            kvx[n].wait_send()

        @pl.when(first)
        def _():
            kvx[0].wait_send()

        sl_f.wait_send()

    @pl.when(xh == 1)
    def _():
        sl_x.wait_send()

    @pl.when(ctx > 0)
    def _():
        s0.wait_send()

    for dr, o in order:
        rs_copy(dr, o).wait_send()


def solution(mesh):
    ny, nz = mesh.shape["head"] // 2, mesh.shape["ctx"] // 4
    lane, hz = 2 * nz, nz // 2

    def body(q, k, v, og, w, sel, cnt):
        rows, width = q.shape
        heads = width // DH
        keys = 4 * rows
        vmem, smem = pl.BlockSpec(memory_space=pltpu.VMEM), pl.BlockSpec(memory_space=pltpu.SMEM)
        dma = pltpu.SemaphoreType.DMA
        scratch = [
            pltpu.VMEM((lane + 3, 2 * rows, DH), BF16),
            pltpu.VMEM((lane, w.shape[1], width), BF16),
            pltpu.VMEM((2, ny, rows, width), BF16),
            pltpu.VMEM((3, 2 * rows, DH), BF16),
            pltpu.VMEM((4, 8, 128), jnp.int32),
            pltpu.SMEM((4, 8, 128), jnp.int32),
            pltpu.VMEM((rows, width), BF16),
            pltpu.VMEM((rows, width), BF16),
            pltpu.VMEM((keys, DH), BF16),
            pltpu.VMEM((keys, DH), BF16),
            pltpu.VMEM((heads, keys, rows), F32),
            pltpu.VMEM((keys, heads * rows), BF16),
            pltpu.VMEM((keys, heads * rows), BF16),
            pltpu.VMEM((heads * rows, DH), BF16),
            pltpu.VMEM((heads * rows, DH), BF16),
            pltpu.VMEM((2 * rows, DH), F32),
            pltpu.VMEM((4, 3, 2 * rows, DH), BF16),
            pltpu.VMEM((2 * rows, DH), BF16),
            pltpu.VMEM((2 * rows, DH), BF16),
            pltpu.VMEM((2, hz, 2 * rows, DH), BF16),
            pltpu.VMEM((2, hz, 2 * rows, DH), BF16),
            dma((2, hz)), dma((2, hz)), dma((nz,)), dma((nz,)),
            dma((2, hz)), dma((2, hz)), dma((nz,)), dma((nz,)),
            dma((2,)), dma((2,)), dma((2, ny - 1)), dma((2, ny - 1)),
            dma((3,)), dma((3,)), dma(()), dma((3,)), dma((3,)),
            dma(()), dma(()), dma((3,)), dma((3,)), dma(()), dma(()),
            dma((2, hz)), dma((2, hz)),
        ]
        return pl.pallas_call(
            functools.partial(kernel, ny, nz),
            out_shape=(
                jax.ShapeDtypeStruct(q.shape, BF16),
                jax.ShapeDtypeStruct(k.shape, BF16),
                jax.ShapeDtypeStruct(v.shape, BF16),
            ),
            in_specs=[vmem] * 5 + [smem] * 2,
            out_specs=(vmem, vmem, vmem),
            scratch_shapes=scratch,
            compiler_params=pltpu.CompilerParams(
                collective_id=0, has_side_effects=True, vmem_limit_bytes=40 << 20
            ),
        )(q, k, v, og, w, sel, cnt)

    placed = P("ctx", "head")
    return jax.shard_map(
        body,
        mesh=mesh,
        in_specs=(placed, placed, placed, placed, P("head", "ctx"), P("head", "ctx", None), P("head", "ctx")),
        out_specs=(placed, placed, placed),
        check_vma=False,
    )
```

time: 561 us -> 89.1 us (0.16)
  waiting for transfers between devices: 163 us -> 0 us
  blocking collectives: 105 us -> 0 us
  starting transfers between devices: 92.9 us -> 0 us
  local copies, waits for them, and re-layouts: 87.8 us -> 3.78 us
  Pallas kernels: 0 us -> 82.9 us
  other arithmetic: 71.4 us -> 0 us
  between operations: 28.2 us -> 1.4 us
  matrix products: 9.57 us -> 0 us
    ppermute x24 -> x0, waiting for transfers between devices: 162 us -> none  [partner_2(): return lax.ppermute(value, axis, pairs)]
    ppermute x24 -> x0, starting transfers between devices: 92.8 us -> none  [partner_2(): return lax.ppermute(value, axis, pairs)]
    pallas_call x0 -> x1, Pallas kernels: none -> 82.9 us  [body(): pl.pallas_call(functools.partial(kernel, ny, nz), out_shape=(jax.ShapeDty...]
    gather x108 -> x0, local copies, waits for them, and re-layouts: 78.4 us -> none  [the longest x64 46.3 us: take_rows(): rows = jnp.take_along_axis(buffer, index[:, :, None, None], axis=1)]
    all_gather x1 -> x0, blocking collectives: 76.3 us -> none  [body(): lax.all_gather(selected, 'ctx', axis=1, tiled=True)]
    unnamed x1 -> x0, blocking collectives: 28.6 us -> none
    another operation x70 -> x0, other arithmetic: 14.1 us -> none  [the longest x24 6.37 us: compact(): rank = jnp.cumsum(member_mask.astype(jnp.int32), axis=1) - 1]
    gather x56 -> x0, other arithmetic: 12.7 us -> none
  transfers between devices with their start and end apart: 26 -> 0, of which waited for: 15 -> 0; matrix products, arithmetic and copies ran while one was open for 24% -> 0% of each run, Pallas kernels for 0% -> 0%
where the time goes in v1:
time: 89.1 us; the launch traced here: 88 us
  Pallas kernels  82.9 us (93%)
  local copies, waits for them, and re-layouts  3.78 us (4%)
  between operations  1.4 us (2%)
    pallas_call x1, Pallas kernels, body(): pl.pallas_call(functools.partial(kernel, ny, nz), out_shape=(jax.ShapeDty...  82.9 us
    unnamed x14, local copies, waits for them, and re-layouts  3.78 us

profile of v1, /device:TPU:1, one launch (start us, length us, event | category | flops | bytes accessed | tf_op | source)
XLA Modules:
  0.0 88.0 jit_solution(3003279528363221990)
XLA Ops:
  0.6 0.0 copy-start
  1.3 0.0 copy-start.2
  1.3 0.0 copy-start.3
  1.3 0.0 copy-start.4
  1.4 1.0 %copy.10.w_ref = bf16[512,64]{1,0:T(8,128)(2,1)S(1)} copy(bf16[512,64]{0,1:T(8,128)(2,1)} %param.11) | data formatting | bytes 131072 | tf_op args[4]
  2.3 0.0 copy-done
  2.3 0.0 copy-done.2
  2.4 0.0 copy-done.3
  2.4 0.0 copy-done.4
  2.4 0.0 copy-start.1
  2.4 0.9 %copy-done.1 = bf16[128,512]{1,0:T(8,128)(2,1)S(1)} copy-done((bf16[128,512]{1,0:T(8,128)(2,1)S(1)}, bf16[128,512]{1,0:T(8,128)(2,1)}, u32[]{:S(2)}) %copy-start.1) | copy-done | bytes 131096
  3.3 82.9 %shard_map.94 = (bf16[128,512]{1,0:T(8,128)(2,1)S(1)}, bf16[128,128]{1,0:T(8,128)(2,1)S(1)}, bf16[128,128]{1,0:T(8,128)(2,1)S(1)}) custom-call(bf16[128,512]{1,0:T(8,128)(2,1)S(1)} %copy-done, bf16[128,128]{1,0:T(8,128)(2,1)S(1)} %copy-done.2, bf16[128,128]{1,0:T(8,128)(2,1)S(1)} %copy-done.3, bf16[128,512]{1,0:T(8,128)(2,1)S(1)} %copy-done.1, ...), custom_call_target="tpu_custom_call" | custom-call | tf_op jit(solution)/shard_map/pallas_call | solution.py:418
  86.1 0.7 copy.15
  86.8 0.6 copy.16
  87.4 0.6 copy.17
Async XLA Ops:
  0.6 1.7 %copy-start = (bf16[128,512]{1,0:T(8,128)(2,1)S(1)}, bf16[128,512]{1,0:T(8,128)(2,1)}, u32[]{:S(2)}) copy-start(bf16[128,512]{1,0:T(8,128)(2,1)} %q_ref.1) | copy-start | bytes 393220
  1.3 1.0 %copy-start.2 = (bf16[128,128]{1,0:T(8,128)(2,1)S(1)}, bf16[128,128]{1,0:T(8,128)(2,1)}, u32[]{:S(2)}) copy-start(bf16[128,128]{1,0:T(8,128)(2,1)} %k_ref.1) | copy-start | bytes 98308
  1.3 1.0 %copy-start.3 = (bf16[128,128]{1,0:T(8,128)(2,1)S(1)}, bf16[128,128]{1,0:T(8,128)(2,1)}, u32[]{:S(2)}) copy-start(bf16[128,128]{1,0:T(8,128)(2,1)} %v_ref.1) | copy-start | bytes 98308
  1.3 1.0 %copy-start.4 = (s32[1,1,3]{2,1,0:T(1,128)S(1)}, s32[1,1,3]{2,1,0:T(1,128)}, u32[]{:S(2)}) copy-start(s32[1,1,3]{2,1,0:T(1,128)} %sel_ref.1) | copy-start | bytes 40
  2.4 0.9 %copy-start.1 = (bf16[128,512]{1,0:T(8,128)(2,1)S(1)}, bf16[128,512]{1,0:T(8,128)(2,1)}, u32[]{:S(2)}) copy-start(bf16[128,512]{1,0:T(8,128)(2,1)} %og_ref.1) | copy-start | bytes 393220

commit v2 on v1

v2 whole, which is shorter than its diff:
```python
import functools

import jax
import jax.numpy as jnp
from jax import lax
from jax.experimental import pallas as pl
from jax.experimental.pallas import tpu as pltpu
from jax.sharding import PartitionSpec as P

MESH = pl.DeviceIdType.MESH
DH = 128
NEG = -1e30
RS_K = 2
OG = (1, 2)
UP = 8
F32 = jnp.float32
BF16 = jnp.bfloat16


def dot(a, b, dims):
    return lax.dot_general(a, b, (dims, ((), ())), preferred_element_type=F32)


NN = ((1,), (0,))
NT = ((1,), (1,))


def kernel(
    ny, nz,
    q_hbm, k_hbm, v_hbm, og_hbm, w_hbm, sel_hbm, cnt_hbm,
    dq_ref, dk_ref, dv_ref,
    q_ref, og_ref, sel_ref, cnt_ref, kvbuf, prev_kv, wbuf, ogbuf, stage, taken, tiles, ids, csend, crecv,
    kall, vall, pfull, plow, dslow, do4, q4, own_sum, pslot_k, pslot_v, s0buf, s0r, sbuf, rbuf, xsend, xrecv,
    in_s, first_s, ring_s, ring_r, share_s, share_r, pk_s, pk_r, ogx_s, ogx_r, ogy_s, ogy_r,
    tile_s, tile_r, ids_s, kvx_s, kvx_r, c_s, c_r, sl_s, sl_r, s0_s, s0_r, rs_s, rs_r, cross_s, cross_r,
):
    lane = 2 * nz
    head, ctx = lax.axis_index("head"), lax.axis_index("ctx")
    xl, y = head // ny, head % ny
    xh, z, c = ctx // lane, (ctx // 2) % nz, ctx % 2
    rows, width = q_ref.shape
    pslot = (pslot_k, pslot_v)
    heads = width // DH
    hops, short, sg = UP, nz - 1 - UP, 2 * c - 1
    longer, mate_longer = c == 1, c == 0

    def at(cx, cz, cc, hd=head):
        return (hd, cx * lane + cz * 2 + cc)

    def zdev(step):
        return at(xh, (z + step + nz) % nz, c)

    def mate(r):
        return at(1 - xh if r & 2 else xh, z, 1 - c if r & 1 else c)

    prev_dev = (head, (ctx + 2 * lane - 1) % (2 * lane))
    next_dev = (head, (ctx + 1) % (2 * lane))
    core_dev = mate(1)

    def remote(src, dst, send, recv, dev):
        return pltpu.make_async_remote_copy(
            src_ref=src, dst_ref=dst, send_sem=send, recv_sem=recv, device_id=dev, device_id_type=MESH
        )

    pending = []

    def go(cp, cond=None):
        pending.append((cond, cp))
        if cond is None:
            cp.start()
        else:
            pl.when(cond)(cp.start)

    me = z * 2 + c
    loads = [
        pltpu.make_async_copy(src, dst, in_s.at[n])
        for n, (src, dst) in enumerate((
            (k_hbm, kvbuf.at[me, 0]), (v_hbm, kvbuf.at[me, 1]), (w_hbm, wbuf.at[me]),
            (og_hbm, og_ref), (sel_hbm, sel_ref), (cnt_hbm, cnt_ref), (q_hbm, q_ref),
        ))
    ]
    barrier = pltpu.get_barrier_semaphore()
    greet = [at(xh, (z + step + nz) % nz, t) for step in (1, -1) for t in (0, 1)]
    greet += [mate(1), mate(2), mate(3), prev_dev, next_dev]
    greet += [zdev(t * n) for n in range(2, RS_K + 1) for t in (1, -1)]
    greet += [((1 - xl) * ny + y, mate(r)[1]) for r in (0, 2)]
    greet += [(xl * ny + (y + dy) % ny, ctx) for dy in range(1, ny)]
    for dev in greet:
        pl.semaphore_signal(barrier, inc=1, device_id=dev, device_id_type=MESH)
    for cp in loads:
        cp.start()
    for cp in loads[:2]:
        cp.wait()
    pl.semaphore_wait(barrier, len(greet))

    half_w = wbuf.shape[1] // 2

    def piece(kind, slot, p):
        return kvbuf.at[slot, p] if kind == 0 else wbuf.at[slot, pl.ds(p * half_w, half_w)]

    def ring(kind, off, ln, p):
        part = piece(kind, ((z - sg * off + nz) % nz) * 2 + ln, p)
        return remote(part, part, ring_s.at[kind, off, ln, p], ring_r.at[kind, off, ln, p], zdev(sg))

    def share(kind, slot_z):
        buf = kvbuf if kind == 0 else wbuf
        part = buf.at[pl.ds(slot_z * 2, 2)]
        return remote(part, part, share_s.at[kind, slot_z], share_r.at[kind, slot_z], core_dev)

    def share_own(kind, core):
        buf = kvbuf if kind == 0 else wbuf
        part = buf.at[z * 2 + core]
        return remote(part, part, share_s.at[kind, z], share_r.at[kind, z], core_dev)

    pieces = [(kind, p) for kind in (0, 1) for p in (0, 1)]
    for kind, p in pieces:
        if (kind, p) == (1, 0):
            loads[2].wait()
        part = piece(kind, me, p)
        for t in (0, 1):
            dev = at(xh, (z + 2 * t - 1 + nz) % nz, t)
            go(remote(part, part, first_s.at[kind, t, p], ring_r.at[kind, 0, c, p], dev))

    pk = remote(kvbuf.at[me], prev_kv, pk_s, pk_r, next_dev)
    go(pk, ctx < 2 * lane - 1)
    for kind in (0, 1):
        go(share_own(kind, c))
    for cp in loads[3:6]:
        cp.wait()

    rel = jnp.where(xh == xl, 0, 1)
    for t in (0, 1):
        cp = remote(og_ref, ogbuf.at[y, rel], ogx_s.at[t], ogx_r.at[rel], at(xl, z, c, t * ny + y))
        go(cp, jnp.logical_not((xh == xl) & (xl == t)))

    row_id = lax.broadcasted_iota(jnp.int32, (8, 128), 0)
    tiles[0] = jnp.where(row_id == 0, sel_ref[0, 0, 1], sel_ref[0, 0, 2])
    tile_cps = [remote(tiles.at[0], tiles.at[r], tile_s.at[r - 1], tile_r.at[r - 1], mate(r)) for r in range(1, 4)]
    for cp in tile_cps:
        go(cp)

    @pl.when(xh == xl)
    def _():
        ogbuf[y, 0] = og_ref[...]

    def ogy(b, dy, slot_y):
        part = ogbuf.at[slot_y, b]
        return remote(part, part, ogy_s.at[b, dy - 1], ogy_r.at[b, dy - 1], (xl * ny + (y + dy) % ny, ctx))

    def when(cond, act):
        if cond is None:
            act()
        else:
            pl.when(cond)(act)

    for off in range(hops):
        here = None if off + 1 <= short else longer
        onward = None if off + 2 <= short else longer
        for kind, p in pieces:
            for ln in (0, 1):
                when(here, ring(kind, off, ln, p).wait_recv)
                if off + 1 < hops:
                    go(ring(kind, off + 1, ln, p), onward)
        for kind in (0, 1):
            go(share(kind, (z - sg * (off + 1) + nz) % nz), here)
        if off == 0:
            loads[6].wait()
            for h in range(heads):
                q4[h * rows : (h + 1) * rows] = q_ref[:, h * DH : (h + 1) * DH]
        if off == 1:
            for n in range(4):
                for kv in (0, 1):
                    pslot[kv][n, 2] = jnp.zeros((rows, DH), BF16)
        for b in (0, 1):
            if off == OG[b]:
                wait = remote(og_ref, ogbuf.at[y, b], ogx_s.at[0], ogx_r.at[b], core_dev).wait_recv
                if b == 0:
                    pl.when(xh != xl)(wait)
                else:
                    wait()
                for dy in range(1, ny):
                    go(ogy(b, dy, y))
        if off == 4:
            for cp in tile_cps:
                cp.wait_recv()
            to_ids = pltpu.make_async_copy(tiles, ids, ids_s)
            to_ids.start()
            to_ids.wait()

    def shared(kind):
        share_own(kind, 1 - c).wait_recv()
        for off in range(hops):
            wait = share(kind, (z + sg * (off + 1) + nz) % nz).wait_recv
            when(None if off + 1 <= short else mate_longer, wait)

    shared(0)

    kvx = []
    for n in (0, 1):
        stage[n] = kvbuf[ids[2, n, 0] % lane]
        kvx.append(remote(stage.at[n], taken.at[n], kvx_s.at[n], kvx_r.at[n], mate(2)))
        go(kvx[n], xh == 0)

    shared(1)
    for b in (0, 1):
        for dy in range(1, ny):
            ogy(b, dy, (y - dy + ny) % ny).wait_recv()

    per = lane // ny

    cols = width // 2

    def project(b, part_col):
        total = None
        for part in range(ny):
            weight = wbuf[part * per : (part + 1) * per, :, part_col * cols : (part_col + 1) * cols].reshape(-1, cols)
            term = dot(ogbuf[part, b], weight, NN)
            total = term if total is None else total + term
        return total

    def cx(n, p):
        part = pl.ds(p * (rows // 2), rows // 2)
        return remote(csend.at[n, part], crecv.at[n, part], c_s.at[n, p], c_r.at[n, p], mate(2))

    for n in (0, 1):
        csend[n] = project(1, n).astype(BF16)
        for p in (0, 1):
            go(cx(n, p))
    own_part = [project(0, n) for n in (0, 1)]

    for cp in kvx:
        pl.when(xh == 1)(cp.wait_recv)
    pl.when(ctx > 0)(pk.wait_recv)

    for n in (0, 1):
        dst = (kall, vall)[n]
        dst[0:rows] = kvbuf[me, n]
        dst[rows : 2 * rows] = prev_kv[n]
    for s in (0, 1):
        b = sel_ref[0, 0, s + 1]
        block = jnp.where(b // lane != xh, taken[s], kvbuf[b % lane])
        kall[(s + 2) * rows : (s + 3) * rows] = block[0]
        vall[(s + 2) * rows : (s + 3) * rows] = block[1]

    scale = DH ** -0.5
    count = cnt_ref[0, 0]

    @pl.when(ctx == 0)
    def _():
        kall[rows : 2 * rows] = jnp.zeros((rows, DH), BF16)
        vall[rows : 2 * rows] = jnp.zeros((rows, DH), BF16)

    key_pos = lax.broadcasted_iota(jnp.int32, (rows, rows), 0)
    tok_pos = lax.broadcasted_iota(jnp.int32, (rows, rows), 1)
    for h in range(heads):
        part = dot(kall[...], q_ref[:, h * DH : (h + 1) * DH], NT) * scale
        parts = [jnp.where(key_pos <= tok_pos, part[0:rows], NEG)]
        for n in range(3):
            parts.append(part[(n + 1) * rows : (n + 2) * rows] + jnp.where(n < count, 0.0, NEG))
        scores = jnp.concatenate(parts, axis=0)
        top = jnp.max(scores, axis=0, keepdims=True)
        raised = jnp.exp(scores - top)
        probs = raised * (1.0 / jnp.sum(raised, axis=0, keepdims=True))
        pfull[h] = probs
        plow[:, h * rows : (h + 1) * rows] = probs.astype(BF16)

    for n in (0, 1):
        for p in (0, 1):
            cx(n, p).wait_recv()
        head_grad = (own_part[n] + crecv[n].astype(F32)).astype(BF16)
        for h in range(heads // 2):
            do4[(n * (heads // 2) + h) * rows : (n * (heads // 2) + h + 1) * rows] = head_grad[:, h * DH : (h + 1) * DH]

    def slots(kv, src, dst, n, dev):
        return [
            remote(pslot[kv].at[src, t], pslot[kv].at[dst, t], sl_s.at[kv, n, t], sl_r.at[kv, n, t], dev)
            for t in (0, 1)
        ]

    def offer(kv, grad):
        own_sum[kv] = grad[0:rows]
        s0buf[kv] = grad[rows : 2 * rows].astype(BF16)
        for s in (0, 1):
            pslot[kv][0, s] = grad[(s + 2) * rows : (s + 3) * rows].astype(BF16)
        for cp in slots(kv, 0, 2, 1, mate(2)):
            go(cp, xh == 1)
        for cp in slots(kv, 0, 1, 0, core_dev):
            go(cp)

    def pass_on(kv):
        for cp, onward in zip(slots(kv, 0, 2, 1, mate(2)), slots(kv, 2, 3, 2, core_dev)):
            pl.when(xh == 0)(cp.wait_recv)
            go(onward, xh == 0)

    def gathered(kv):
        for cp in slots(kv, 0, 1, 0, core_dev):
            cp.wait_recv()
        for cp in slots(kv, 2, 3, 2, core_dev):
            pl.when(xh == 0)(cp.wait_recv)

    offer(1, dot(plow[...], do4[...], NN))
    for h in range(heads):
        grad_probs = dot(vall[...], do4[h * rows : (h + 1) * rows], NT)
        low = plow[:, h * rows : (h + 1) * rows].astype(F32)
        delta = jnp.sum(low * grad_probs, axis=0, keepdims=True)
        dslow[:, h * rows : (h + 1) * rows] = (pfull[h] * (grad_probs - delta)).astype(BF16)
    offer(0, dot(dslow[...], q4[...], NN))
    s0 = remote(s0buf, s0r, s0_s, s0_r, prev_dev)
    go(s0, ctx > 0)
    pass_on(1)

    key_t = kall[...].T
    for h in range(heads):
        part = dot(key_t, dslow[:, h * rows : (h + 1) * rows], NN) * scale
        dq_ref[:, h * DH : (h + 1) * DH] = part.T.astype(BF16)

    wanted = [(sel_ref[0, 0, 1], sel_ref[0, 0, 2])] + [(ids[r, 0, 0], ids[r, 1, 0]) for r in range(1, 4)]

    def contribution(kv, slot_z, ln):
        target = xh * lane + slot_z * 2 + ln
        total = None
        for r, (one, two) in enumerate(wanted):
            index = jnp.where(one == target, 0, jnp.where(two == target, 1, 2))
            term = pslot[kv][r, index].astype(F32)
            total = term if total is None else total + term
        return total

    def rs_copy(kv, o, ln):
        sems = rs_s.at[kv, o - 1, ln], rs_r.at[kv, o - 1, ln]
        dev = zdev(sg * (o % RS_K or RS_K))
        return remote(sbuf.at[kv, o - 1, ln], rbuf.at[kv, o - 1, ln], *sems, dev)

    def rs_collect(total, kv, o, ln):
        for o2 in range(min(o + RS_K, hops), o, -1):
            if o2 <= short:
                rs_copy(kv, o2, ln).wait_recv()
                total = total + rbuf[kv, o2 - 1, ln].astype(F32)
            else:
                pl.when(longer)(rs_copy(kv, o2, ln).wait_recv)
                total = total + jnp.where(longer, rbuf[kv, o2 - 1, ln].astype(F32), 0.0)
        return total

    def rs_send(kv, o):
        for ln in (0, 1):
            total = contribution(kv, (z + sg * o + nz) % nz, ln)
            if o % RS_K == 0:
                total = rs_collect(total, kv, o, ln)
            sbuf[kv, o - 1, ln] = total.astype(BF16)
            go(rs_copy(kv, o, ln), None if o <= short else longer)

    late = [o for p in range(hops - 2, 0, -2) for o in (p - 1, p)]

    gathered(1)
    for o in (hops, hops - 1):
        rs_send(1, o)
    pass_on(0)
    gathered(0)
    for o in (hops, hops - 1):
        rs_send(0, o)
    for o in late:
        for kv in (1, 0):
            rs_send(kv, o)

    pl.when(ctx < 2 * lane - 1)(s0.wait_recv)
    cross = [remote(xsend.at[kv], xrecv.at[kv], cross_s.at[kv], cross_r.at[kv], core_dev) for kv in (0, 1)]
    for kv in (1, 0):
        zero = jnp.zeros((rows, DH), F32)
        ends = [rs_collect(zero, kv, 0, ln) for ln in (0, 1)]
        xsend[kv] = jnp.where(c == 0, ends[1], ends[0]).astype(BF16)
        go(cross[kv])
        total = own_sum[kv] + contribution(kv, z, c) + jnp.where(c == 0, ends[0], ends[1])
        own_sum[kv] = total + jnp.where(ctx < 2 * lane - 1, s0r[kv].astype(F32), 0.0)
    for kv in (1, 0):
        cross[kv].wait_recv()
        total = own_sum[kv] + xrecv[kv].astype(F32)
        if kv == 1:
            dv_ref[...] = total.astype(BF16)
        else:
            dk_ref[...] = (total * scale).astype(BF16)

    for cond, cp in pending:
        if cond is None:
            cp.wait_send()
        else:
            pl.when(cond)(cp.wait_send)


def solution(mesh):
    ny, nz = mesh.shape["head"] // 2, mesh.shape["ctx"] // 4
    lane = 2 * nz

    def body(q, k, v, og, w, sel, cnt):
        rows, width = q.shape
        heads = width // DH
        keys = 4 * rows
        vmem, hbm = pl.BlockSpec(memory_space=pltpu.VMEM), pl.BlockSpec(memory_space=pltpu.HBM)
        dma = pltpu.SemaphoreType.DMA
        scratch = [
            pltpu.VMEM(q.shape, BF16),
            pltpu.VMEM(og.shape, BF16),
            pltpu.SMEM(sel.shape, jnp.int32),
            pltpu.SMEM(cnt.shape, jnp.int32),
            pltpu.VMEM((lane, 2, rows, DH), BF16),
            pltpu.VMEM((2, rows, DH), BF16),
            pltpu.VMEM((lane, w.shape[1], width), BF16),
            pltpu.VMEM((ny, 2, rows, width), BF16),
            pltpu.VMEM((2, 2, rows, DH), BF16),
            pltpu.VMEM((2, 2, rows, DH), BF16),
            pltpu.VMEM((4, 8, 128), jnp.int32),
            pltpu.SMEM((4, 8, 128), jnp.int32),
            pltpu.VMEM((2, rows, width // 2), BF16),
            pltpu.VMEM((2, rows, width // 2), BF16),
            pltpu.VMEM((keys, DH), BF16),
            pltpu.VMEM((keys, DH), BF16),
            pltpu.VMEM((heads, keys, rows), F32),
            pltpu.VMEM((keys, heads * rows), BF16),
            pltpu.VMEM((keys, heads * rows), BF16),
            pltpu.VMEM((heads * rows, DH), BF16),
            pltpu.VMEM((heads * rows, DH), BF16),
            pltpu.VMEM((2, rows, DH), F32),
            pltpu.VMEM((4, 3, rows, DH), BF16),
            pltpu.VMEM((4, 3, rows, DH), BF16),
            pltpu.VMEM((2, rows, DH), BF16),
            pltpu.VMEM((2, rows, DH), BF16),
            pltpu.VMEM((2, UP, 2, rows, DH), BF16),
            pltpu.VMEM((2, UP, 2, rows, DH), BF16),
            pltpu.VMEM((2, rows, DH), BF16),
            pltpu.VMEM((2, rows, DH), BF16),
            dma((7,)),
            dma((2, 2, 2)), dma((2, UP, 2, 2)), dma((2, UP, 2, 2)),
            dma((2, nz)), dma((2, nz)),
            dma(()), dma(()),
            dma((2,)), dma((2,)), dma((2, ny - 1)), dma((2, ny - 1)),
            dma((3,)), dma((3,)), dma(()), dma((2,)), dma((2,)),
            dma((2, 2)), dma((2, 2)), dma((2, 3, 2)), dma((2, 3, 2)), dma(()), dma(()),
            dma((2, UP, 2)), dma((2, UP, 2)), dma((2,)), dma((2,)),
        ]
        return pl.pallas_call(
            functools.partial(kernel, ny, nz),
            out_shape=(
                pltpu.VMEM(q.shape, BF16),
                pltpu.VMEM(k.shape, BF16),
                pltpu.VMEM(v.shape, BF16),
            ),
            in_specs=[hbm] * 7,
            out_specs=(vmem, vmem, vmem),
            scratch_shapes=scratch,
            compiler_params=pltpu.CompilerParams(
                collective_id=0, has_side_effects=True, vmem_limit_bytes=60 << 20
            ),
        )(q, k, v, og, w.T, sel, cnt)

    placed = P("ctx", "head")
    return jax.shard_map(
        body,
        mesh=mesh,
        in_specs=(placed, placed, placed, placed, P("head", "ctx"), P("head", "ctx", None), P("head", "ctx")),
        out_specs=(placed, placed, placed),
        check_vma=False,
    )
```

time: 89.1 us -> 79.2 us (0.89); the launches traced: 88 us -> 79.1 us
  Pallas kernels: 82.9 us -> 75.9 us
  local copies, waits for them, and re-layouts: 3.78 us -> 1.89 us
    pallas_call x1, Pallas kernels: 82.9 us -> 75.9 us  [body(): pl.pallas_call(functools.partial(kernel, ny, nz), out_shape=(pltpu.VMEM(q...]
    unnamed x14 -> x3, local copies, waits for them, and re-layouts: 3.78 us -> 1.89 us
where the time goes in v2:
time: 79.2 us; the launch traced here: 79.1 us
  Pallas kernels  75.9 us (96%)
  local copies, waits for them, and re-layouts  1.89 us (2%)
  between operations  1.29 us (2%)
    pallas_call x1, Pallas kernels, body(): pl.pallas_call(functools.partial(kernel, ny, nz), out_shape=(pltpu.VMEM(q...  75.9 us
    unnamed x3, local copies, waits for them, and re-layouts  1.89 us

profile of v2, /device:TPU:1, one launch (start us, length us, event | category | flops | bytes accessed | tf_op | source)
XLA Modules:
  0.0 79.1 jit_solution(12938215624705494930)
XLA Ops:
  1.3 75.9 %shard_map.94 = (bf16[128,512]{1,0:T(8,128)(2,1)S(1)}, bf16[128,128]{1,0:T(8,128)(2,1)S(1)}, bf16[128,128]{1,0:T(8,128)(2,1)S(1)}) custom-call(bf16[128,512]{1,0:T(8,128)(2,1)} %q_hbm.1, bf16[128,128]{1,0:T(8,128)(2,1)} %k_hbm.1, bf16[128,128]{1,0:T(8,128)(2,1)} %v_hbm.1, bf16[128,512]{1,0:T(8,128)(2,1)} %og_hbm.1, bf16[64,512]{1,0:T(8,128)(2,1)} %bitcast.1, ...), custom_call_target="tpu_custom_call" | custom-call | tf_op jit(solution)/shard_map/pallas_call | solution.py:438
  77.2 0.7 copy.13
  77.9 0.6 copy.14
  78.5 0.6 copy.15
